TPU v7x, 32 devices: a whole 2x2x4 slice. The times are simulated.
32 devices in a mesh: seq: 16 (over z, y, core), head: 2 (over x).
Axes of the slice: x: 2, y: 2, z: 4, core: 2. Of those that a mesh axis runs over, the one named last changes fastest.
Arguments:
- query_key: bfloat16 [8192, 2048], P('seq', 'head'), may hold values from -7 to 7
- values: bfloat16 [8192, 2048], P('seq', 'head'), may hold values from -12 to 12
- out_weight: bfloat16 [2048, 2048], P('head'), may hold values from -0.125 to 0.125
- out_grad: bfloat16 [8192, 2048], P('seq'), may hold values from -12 to 12
- sort_order: int32 [16, 8192], P('head', 'seq'), may hold values from 0 to 8191, as said below
- undo_order: int32 [16, 8192], P('head', 'seq'), may hold values from 0 to 8191, as said below
Outputs:
- projected: bfloat16 [8192, 2048], P('seq', 'head')
- shared_grad: bfloat16 [8192, 2048], P('seq', 'head')
- value_grad: bfloat16 [8192, 2048], P('seq', 'head')
Inputs may be any that keep to these rules, and one draw needn't show every extreme that they name: `sort_order`: each row holds every token index once. For every head, among the tokens t with t // 512 = a, at most 48 have bucket positions p with p // 512 = b, for every pair a, b; exactly 48 for some pair. undo_order[h, sort_order[h, p]] = p for every head h and position p.
All inputs are finite; a program needn't handle non-finite values.
Results may differ from a plain program's by a relative error of at most 0.0079.
Values may be sent and summed in bfloat16 or wider, within the bound.
A program may use at most 128 MiB of HBM per device.

v0:
```python
import jax
import jax.numpy as jnp
from jax import lax
from jax.sharding import PartitionSpec as P

GROUP = 256


NORM_EPS = 1e-06


def from_behind(x, axis, by):
    devices = lax.axis_size(axis)
    return lax.ppermute(x, axis, [(i, (i + by) % devices) for i in range(devices)])


def send_table(undo_order, tok_dev, capacity, slots):
    target = undo_order // tok_dev
    same_target = target[:, :, None] == target[:, None, :]
    before = undo_order[:, None, :] < undo_order[:, :, None]
    rank = jnp.sum((same_target & before).astype(jnp.int32), axis=2)
    outbound = target * capacity + rank
    slot_ids = jnp.arange(slots, dtype=jnp.int32)
    return (outbound[:, None, :] == slot_ids[None, :, None]).astype(jnp.bfloat16)


def receive_table(sort_order, tok_dev, capacity, slots):
    source = sort_order // tok_dev
    same_source = source[:, :, None] == source[:, None, :]
    places = jnp.arange(tok_dev, dtype=jnp.int32)
    earlier = places[None, :] < places[:, None]
    rank = jnp.sum((same_source & earlier[None]).astype(jnp.int32), axis=2)
    inbound = source * capacity + rank
    slot_ids = jnp.arange(slots, dtype=jnp.int32)
    return (inbound[:, :, None] == slot_ids[None, None, :]).astype(jnp.bfloat16)


def on_device(query_key, values, out_weight, out_grad, sort_order, undo_order):
    tok_dev = query_key.shape[0]
    head_count = sort_order.shape[0]
    head_size = query_key.shape[1] // head_count
    devices = lax.axis_size("seq")
    capacity = 3 * tok_dev // (2 * devices)
    slots = devices * capacity
    block_len = GROUP
    blocks = tok_dev // block_len
    score_scale = head_size ** (-0.5)
    outgoing = send_table(undo_order, tok_dev, capacity, slots)
    incoming = receive_table(sort_order, tok_dev, capacity, slots)

    def pack_tokens(rows):
        packed = jnp.einsum(
            "hst,thf->shf", outgoing, rows, preferred_element_type=jnp.float32
        ).astype(jnp.bfloat16)
        return packed.reshape(devices, capacity, head_count, rows.shape[2])

    def unpack_positions(buffer):
        flat = buffer.reshape(slots, head_count, buffer.shape[3])
        return jnp.einsum(
            "hps,shf->phf", incoming, flat, preferred_element_type=jnp.float32
        ).astype(jnp.bfloat16)

    row_shape = (tok_dev, head_count, head_size)
    block_shape = (blocks, block_len, head_count, head_size)
    attended_grad = lax.dot_general(
        out_grad, out_weight, (((1,), (1,)), ((), ())), preferred_element_type=jnp.float32
    ).astype(jnp.bfloat16)
    query_tok = query_key.reshape(row_shape)
    value_tok = values.reshape(row_shape)
    grad_tok = attended_grad.reshape(row_shape)
    stacked = pack_tokens(jnp.concatenate([query_tok, value_tok], axis=2))
    arrived = unpack_positions(
        lax.all_to_all(stacked, "seq", split_axis=0, concat_axis=0, tiled=True)
    )
    query_blocks = arrived[:, :, :head_size].reshape(block_shape)
    value_blocks = arrived[:, :, head_size : 2 * head_size].reshape(block_shape)
    query_wide = query_blocks.astype(jnp.float32)
    inverse_norm = lax.rsqrt(jnp.mean(query_wide * query_wide, axis=3, keepdims=True) + NORM_EPS)
    key_blocks = (query_wide * inverse_norm).astype(jnp.bfloat16)
    prior = from_behind((key_blocks[-1], value_blocks[-1]), "seq", 1)
    key_window = jnp.concatenate(
        [jnp.concatenate([prior[0][None], key_blocks[:-1]], axis=0), key_blocks], axis=1
    )
    value_window = jnp.concatenate(
        [jnp.concatenate([prior[1][None], value_blocks[:-1]], axis=0), value_blocks], axis=1
    )
    scores = (
        jnp.einsum("nqhd,nkhd->nhqk", query_blocks, key_window, preferred_element_type=jnp.float32)
        * score_scale
    )
    keep_mask = jnp.arange(2 * block_len)[None, :] != jnp.arange(block_len)[:, None] + block_len
    weights = jnp.where(keep_mask, jnp.exp(scores), 0.0)
    probability = (weights / jnp.sum(weights, axis=3, keepdims=True)).astype(jnp.bfloat16)
    out_blocks = jnp.einsum(
        "nhqk,nkhd->nqhd", probability, value_window, preferred_element_type=jnp.float32
    ).astype(jnp.bfloat16)
    grad_packed = pack_tokens(grad_tok)
    grad_blocks = unpack_positions(
        lax.all_to_all(grad_packed, "seq", split_axis=0, concat_axis=0, tiled=True)
    ).reshape(block_shape)
    prob_grad = jnp.einsum(
        "nqhd,nkhd->nhqk", grad_blocks, value_window, preferred_element_type=jnp.float32
    )
    prob_wide = probability.astype(jnp.float32)
    row_delta = jnp.sum(prob_wide * prob_grad, axis=3, keepdims=True)
    score_grad = (prob_wide * (prob_grad - row_delta) * score_scale).astype(jnp.bfloat16)
    value_window_grad = jnp.einsum(
        "nhqk,nqhd->nkhd", probability, grad_blocks, preferred_element_type=jnp.float32
    )
    query_grad = jnp.einsum(
        "nhqk,nkhd->nqhd", score_grad, key_window, preferred_element_type=jnp.float32
    )
    key_window_grad = jnp.einsum(
        "nhqk,nqhd->nkhd", score_grad, query_blocks, preferred_element_type=jnp.float32
    )
    passed = (
        from_behind(key_window_grad[0, :block_len].astype(jnp.bfloat16), "seq", -1).astype(
            jnp.float32
        ),
        from_behind(value_window_grad[0, :block_len].astype(jnp.bfloat16), "seq", -1).astype(
            jnp.float32
        ),
    )
    key_grad = key_window_grad[:, block_len:] + jnp.concatenate(
        [key_window_grad[1:, :block_len], passed[0][None]], axis=0
    )
    value_sum = value_window_grad[:, block_len:] + jnp.concatenate(
        [value_window_grad[1:, :block_len], passed[1][None]], axis=0
    )
    sorted_value_grad = value_sum.astype(jnp.bfloat16)
    inner = jnp.sum(key_grad * query_wide, axis=3, keepdims=True)
    cubed = inverse_norm * inverse_norm * inverse_norm
    sorted_shared_grad = (
        query_grad + inverse_norm * key_grad - cubed * query_wide * inner / head_size
    ).astype(jnp.bfloat16)
    results = jnp.concatenate(
        [
            out_blocks.reshape(row_shape),
            sorted_shared_grad.reshape(row_shape),
            sorted_value_grad.reshape(row_shape),
        ],
        axis=2,
    )
    packed = jnp.einsum(
        "hps,phf->shf", incoming, results, preferred_element_type=jnp.float32
    ).astype(jnp.bfloat16)
    buffer = lax.all_to_all(
        packed.reshape(devices, capacity, head_count, results.shape[2]),
        "seq",
        split_axis=0,
        concat_axis=0,
        tiled=True,
    )
    flat = buffer.reshape(slots, head_count, buffer.shape[3])
    returned = jnp.einsum(
        "hst,shf->thf", outgoing, flat, preferred_element_type=jnp.float32
    ).astype(jnp.bfloat16)
    flat_width = head_count * head_size
    attended = returned[:, :, :head_size].reshape(tok_dev, flat_width)
    shared_grad = returned[:, :, head_size : 2 * head_size].reshape(tok_dev, flat_width)
    value_grad = returned[:, :, 2 * head_size :].reshape(tok_dev, flat_width)
    partial_terms = jnp.dot(attended, out_weight, preferred_element_type=jnp.float32)
    projected = lax.psum_scatter(partial_terms, "head", scatter_dimension=1, tiled=True).astype(
        jnp.bfloat16
    )
    return (projected, shared_grad, value_grad)


def solution(mesh):
    placed = (
        P("seq", "head"),
        P("seq", "head"),
        P("head", None),
        P("seq", None),
        P("head", "seq"),
        P("head", "seq"),
    )
    return jax.shard_map(
        on_device,
        mesh=mesh,
        in_specs=placed,
        out_specs=(P("seq", "head"), P("seq", "head"), P("seq", "head")),
        check_vma=False,
    )
```

profile of v0, /device:TPU:0, one launch (start us, length us, event | category | flops | bytes accessed | tf_op | source)
XLA Modules:
  0.0 424.0 jit_solution(17454268405549455761)
XLA Ops:
  7.2 0.9 add_select_fusion.1
  8.1 2.9 convert_reduce_fusion.1
  11.0 0.7 multiply_add_fusion.1
  11.7 1.5 copy.52
  13.2 2.3 copy.51
  15.5 5.7 %convert_bitcast_fusion.2 = bf16[768,8,256]{0,2,1:T(8,128)(2,1)} fusion(s32[8,512]{1,0:T(8,128)S(1)} %multiply_add_fusion.1, bf16[512,8,128]{0,2,1:T(8,128)(2,1)S(1)} %bitcast.88, bf16[512,8,128]{0,2,1:T(8,128)(2,1)} %bitcast.89), kind=kOutput, calls=%fused_computation.40 | convolution fusion | flops 1619525632 | bytes 5259264 | tf_op jit(solution)/shard_map/hst,thf->shf/dot_general | solution.py:52
  21.2 5.1 %copy.53 = bf16[768,8,256]{2,1,0:T(8,128)(2,1)} copy(bf16[768,8,256]{0,2,1:T(8,128)(2,1)} %convert_bitcast_fusion.2) | data formatting | bytes 6291456 | tf_op jit(solution)/shard_map/convert_element_type | solution.py:54
  26.3 7.4 %all-to-all-start = ((bf16[16,48,8,256]{3,2,1,0:T(8,128)(2,1)}), bf16[16,48,8,256]{3,2,1,0:T(8,128)(2,1)}, u32[]{:S(2)}, u32[]{:S(2)}) async-start(bf16[16,48,8,256]{3,2,1,0:T(8,128)(2,1)} %bitcast.75), calls=%async_computation | async-start | bytes 6291456 | tf_op jit(solution)/shard_map/all_to_all | solution.py:73
  33.8 5.5 %convolution_convert_fusion.1 = bf16[512,1024]{1,0:T(8,128)(2,1)} fusion(bf16[512,2048]{1,0:T(8,128)(2,1)S(1)} %copy-done, bf16[1024,2048]{1,0:T(8,128)(2,1)} %param.8), kind=kOutput, calls=%fused_computation.64 | convolution fusion | flops 2148007936 | bytes 7340032 | tf_op jit(solution)/shard_map/dot_general | solution.py:65
  39.3 1.5 copy.82
  40.8 2.8 fusion.45
  43.6 2.0 copy.60
  45.6 47.6 %all-to-all-done = bf16[16,48,8,256]{3,2,1,0:T(8,128)(2,1)} async-done(((bf16[16,48,8,256]{3,2,1,0:T(8,128)(2,1)}), bf16[16,48,8,256]{3,2,1,0:T(8,128)(2,1)}, u32[]{:S(2)}, u32[]{:S(2)}) %all-to-all-start) | async-done | bytes 3145760 | tf_op jit(solution)/shard_map/all_to_all | solution.py:73
  93.2 15.5 %all-to-all-start.1 = ((bf16[16,48,8,128]{3,2,1,0:T(8,128)(2,1)}), bf16[16,48,8,128]{3,2,1,0:T(8,128)(2,1)}, u32[]{:S(2)}, u32[]{:S(2)}) async-start(bf16[16,48,8,128]{3,2,1,0:T(8,128)(2,1)} %bitcast.15), calls=%async_computation.1 | async-start | bytes 3145728 | tf_op jit(solution)/shard_map/all_to_all | solution.py:99
  108.7 0.2 reduce-scatter.2.cloned.1.call-start
  109.0 2.2 convert_reduce_fusion
  111.3 0.1 iota_compare_fusion.23
  111.4 5.7 %convert_bitcast_fusion.3 = bf16[512,8,256]{0,2,1:T(8,128)(2,1)S(1)} fusion(s32[8,512]{1,0:T(8,128)S(1)} %multiply_add_fusion, bf16[768,8,256]{2,1,0:T(8,128)(2,1)} %bitcast.4), kind=kOutput, calls=%fused_computation.58 | convolution fusion | flops 1614807040 | bytes 5259264 | tf_op jit(solution)/shard_map/hps,shf->phf/dot_general | solution.py:59
  117.1 1.2 fusion.76
  118.3 1.1 reshape.123
  119.4 2.5 copy.57
  121.9 0.2 multiply_reduce_fusion
  122.2 0.7 fusion.32
  122.9 1.0 copy-done.5
  123.9 1.0 slice_bitcast_fusion
  124.9 0.4 collective-permute-start.1
  125.3 21.1 %all-to-all-done.1 = bf16[16,48,8,128]{3,2,1,0:T(8,128)(2,1)} async-done(((bf16[16,48,8,128]{3,2,1,0:T(8,128)(2,1)}), bf16[16,48,8,128]{3,2,1,0:T(8,128)(2,1)}, u32[]{:S(2)}, u32[]{:S(2)}) %all-to-all-start.1) | async-done | bytes 1572896 | tf_op jit(solution)/shard_map/all_to_all | solution.py:99
  146.3 4.4 %fusion.46 = bf16[8,128,512]{2,1,0:T(8,128)(2,1)S(1)} fusion(s32[8,512]{1,0:T(8,128)S(1)} %multiply_add_fusion, bf16[768,8,128]{2,1,0:T(8,128)(2,1)} %bitcast.16), kind=kOutput, calls=%fused_computation.63 | convolution fusion | flops 808976384 | bytes 2637824 | tf_op jit(solution)/shard_map/hps,shf->phf/dot_general | solution.py:59
  150.9 1.0 collective-permute-start
  152.1 3.2 fusion.10
  155.3 1.7 divide_convert_fusion
  157.0 0.7 convolution_bitcast_fusion
  157.9 2.3 copy-done.3
  160.2 0.9 fusion.58
  161.1 1.4 collective-permute-done
  162.5 4.5 %fusion.51 = f32[2,8,256,512]{3,2,1,0:T(8,128)} fusion(bf16[8,16,2,8,256]{4,3,2,1,0:T(8,128)(2,1)S(1)} %bitcast.85, bf16[2,256,8,128]{1,3,2,0:T(8,128)(2,1)S(1)} %bitcast.86, bf16[1,256,8,128]{1,3,2,0:T(8,128)(2,1)S(1)} %get-tuple-element.16, bf16[1,256,8,128]{1,3,2,0:T(8,128)(2,1)S(1)} %bitcast.91), kind=kOutput, calls=%fused_computation.67 | convolution fusion | flops 543162368 | bytes 11534336 | tf_op jit(solution)/shard_map/nqhd,nkhd->nhqk/dot_general | solution.py:101
  167.0 2.5 fusion.50
  169.5 2.2 collective-permute-start.3
  171.7 12.9 %fusion.31 = f32[2,512,8,128]{3,1,2,0:T(8,128)} fusion(bf16[2,256,8,128]{3,1,2,0:T(8,128)(2,1)S(1)} %copy.57, bf16[2,8,256,512]{3,2,1,0:T(8,128)(2,1)} %copy-done.2, f32[2,8,256,512]{3,2,1,0:T(8,128)} %fusion.51), kind=kOutput, calls=%fused_computation.41 | convolution fusion | flops 551555584 | bytes 17825792 | tf_op jit(solution)/shard_map/nhqk,nqhd->nkhd/dot_general | solution.py:113
  184.6 1.3 slice.76
  185.9 2.1 fusion.57
  188.0 0.2 collective-permute-start.2
  188.2 2.4 copy.58
  190.6 2.4 copy.71
  193.1 12.3 %fusion.20 = f32[2,8,128,256]{2,3,1,0:T(8,128)} fusion(bf16[2,8,256,512]{3,2,1,0:T(8,128)(2,1)} %copy-done.2, f32[2,8,256,512]{3,2,1,0:T(8,128)} %fusion.51, bf16[2,256,8,128]{3,1,2,0:T(8,128)(2,1)} %copy-done.5, bf16[1,256,8,128]{3,1,2,0:T(8,128)(2,1)} %get-tuple-element.20, bf16[1,256,8,128]{3,1,2,0:T(8,128)(2,1)} %bitcast.10), kind=kOutput, calls=%fused_computation.29 | convolution fusion | flops 557847040 | bytes 16777216 | tf_op jit(solution)/shard_map/nhqk,nkhd->nqhd/dot_general | solution.py:110
  205.4 1.1 bitcast_convert_fusion
  206.6 2.9 fusion.37
  209.4 1.7 copy.70
  211.1 1.5 copy.73
  212.6 1.1 bitcast_convert_fusion.1
  213.7 9.7 %fusion.36 = bf16[2,256,8,128]{3,1,2,0:T(8,128)(2,1)S(1)} fusion(bf16[2,256,8,128]{3,1,2,0:T(8,128)(2,1)S(1)} %copy.57, f32[2,8,128,256]{2,3,1,0:T(8,128)} %fusion.20, f32[2,256,8]{1,2,0:T(8,128)S(1)} %multiply_multiply_fusion, f32[2,256,8]{1,2,0:T(8,128)S(1)} %bitcast.95, f32[1,256,8,128]{3,1,2,0:T(8,128)S(1)} %bitcast_convert_fusion.1, ...), kind=kOutput, calls=%fused_computation.47 | output fusion | flops 7344255 | bytes 13664256 | tf_op jit(solution)/shard_map/mul | solution.py:134
  223.4 0.7 copy.68
  224.1 1.5 copy.72
  225.6 5.7 %convert_bitcast_fusion = bf16[768,8,384]{0,2,1:T(8,128)(2,1)} fusion(s32[8,512]{1,0:T(8,128)S(1)} %multiply_add_fusion, bf16[512,8,128]{0,2,1:T(8,128)(2,1)S(1)} %copy-done.9, bf16[512,8,128]{0,2,1:T(8,128)(2,1)} %copy.72, bf16[512,8,128]{0,2,1:T(8,128)(2,1)S(1)} %copy-done.8), kind=kOutput, calls=%fused_computation.27 | convolution fusion | flops 2430861312 | bytes 7880704 | tf_op jit(solution)/shard_map/hps,phf->shf/dot_general | solution.py:144
  231.3 7.1 %copy.74 = bf16[768,8,384]{2,1,0:T(8,128)(2,1)} copy(bf16[768,8,384]{0,2,1:T(8,128)(2,1)} %convert_bitcast_fusion) | data formatting | bytes 9437184 | tf_op jit(solution)/shard_map/convert_element_type | solution.py:146
  238.4 110.0 %all_to_all.15 = bf16[16,48,8,384]{3,2,1,0:T(8,128)(2,1)S(1)} all-to-all(bf16[16,48,8,384]{3,2,1,0:T(8,128)(2,1)} %bitcast.74), channel_id=1, replica_groups=mesh['seq'=16,'head'=2] {'seq'}, dimensions={0} | all-to-all | bytes 9437184 | tf_op jit(solution)/shard_map/all_to_all | solution.py:147
  348.4 3.4 convert_bitcast_fusion.1
  351.8 1.3 fusion.74
  353.1 1.3 copy-done.4
  354.4 4.4 %fusion.77 = f32[512,2048]{1,0:T(8,128)} fusion(bf16[512,1024]{0,1:T(8,128)(2,1)S(1)} %bitcast.76, bf16[1024,2048]{1,0:T(8,128)(2,1)S(1)} %copy-done.4), kind=kOutput, calls=%fused_computation.117 | convolution fusion | flops 2147483648 | bytes 9437184 | tf_op jit(solution)/shard_map/dot_general | solution.py:162
  358.8 2.4 copy.76
  361.2 1.3 copy.77
  362.5 51.4 %reduce-scatter.2.cloned.1.call-done = f32[512,1024]{1,0:T(8,128)} async-done(((f32[512,2048]{1,0:T(8,128)}), f32[512,1024]{1,0:T(8,128)}) %reduce-scatter.2.cloned.1.call-update) | async-done | bytes 2097168 | tf_op jit(solution)/shard_map/reduce_scatter | solution.py:163
  413.9 2.7 convert_element_type.117
  (34 shorter events, 0.6 us)
Async XLA Ops:
  7.2 26.6 %copy-start = (bf16[512,2048]{1,0:T(8,128)(2,1)S(1)}, bf16[512,2048]{1,0:T(8,128)(2,1)}, u32[]{:S(2)}) copy-start(bf16[512,2048]{1,0:T(8,128)(2,1)} %param.9) | copy-start | bytes 6291460
  26.3 66.9 %all-to-all-start = ((bf16[16,48,8,256]{3,2,1,0:T(8,128)(2,1)}), bf16[16,48,8,256]{3,2,1,0:T(8,128)(2,1)}, u32[]{:S(2)}, u32[]{:S(2)}) async-start(bf16[16,48,8,256]{3,2,1,0:T(8,128)(2,1)} %bitcast.75), calls=%async_computation | async-start | bytes 6291456 | tf_op jit(solution)/shard_map/all_to_all | solution.py:73
  43.6 65.4 %copy-start.11 = (s32[8,512]{1,0:T(8,128)S(1)}, s32[8,512]{1,0:T(8,128)}, u32[]{:S(2)}) copy-start(s32[8,512]{1,0:T(8,128)} %param.10) | copy-start | bytes 49156
  93.2 53.1 %all-to-all-start.1 = ((bf16[16,48,8,128]{3,2,1,0:T(8,128)(2,1)}), bf16[16,48,8,128]{3,2,1,0:T(8,128)(2,1)}, u32[]{:S(2)}, u32[]{:S(2)}) async-start(bf16[16,48,8,128]{3,2,1,0:T(8,128)(2,1)} %bitcast.15), calls=%async_computation.1 | async-start | bytes 3145728 | tf_op jit(solution)/shard_map/all_to_all | solution.py:99
  108.7 305.2 %reduce-scatter.2.cloned.1.call-start = ((), (), s32[]{:S(2)}) async-start(), calls=%async_computation.4 | async-start | bytes 6291456 | tf_op jit(solution)/shard_map/reduce_scatter | solution.py:163
  122.9 1.0 copy-start.5
  124.9 27.1 %collective-permute-start.1 = (bf16[256,8,128]{2,0,1:T(8,128)(2,1)}, bf16[256,8,128]{2,0,1:T(8,128)(2,1)}, u32[]{:S(2)}, u32[]{:S(2)}) collective-permute-start(bf16[256,8,128]{2,0,1:T(8,128)(2,1)} %get-tuple-element.19), channel_id=1, source_target_pairs={{0,2},{2,4},{4,6},{6,8},{8,10},{10,12},{12,14},{14,16},{16,18},{18... | collective-permute-start | bytes 1572872 | tf_op jit(solution)/shard_map/ppermute | solution.py:14
  146.3 4.4 %copy-start.7 = (bf16[512,8,128]{0,2,1:T(8,128)(2,1)S(1)}, bf16[512,8,128]{0,2,1:T(8,128)(2,1)}, u32[]{:S(2)}) copy-start(bf16[512,8,128]{0,2,1:T(8,128)(2,1)} %get-tuple-element.17) | copy-start | bytes 3145732
  150.7 1.3 copy-start.6
  150.7 1.3 copy-start.10
  150.9 11.6 %collective-permute-start = (bf16[256,8,128]{0,2,1:T(8,128)(2,1)S(1)}, bf16[256,8,128]{0,2,1:T(8,128)(2,1)S(1)}, u32[]{:S(2)}, u32[]{:S(2)}) collective-permute-start(bf16[256,8,128]{0,2,1:T(8,128)(2,1)S(1)} %get-tuple-element.15), channel_id=1, source_target_pairs={{0,2},{2,4},{4,6},{6,8},{8,10},{10,12},{12,14},{14,16},{16,18},{18... | collective-permute-start | bytes 1572872 | tf_op jit(solution)/shard_map/ppermute | solution.py:14
  157.0 10.0 %copy-start.2 = (bf16[2,8,256,512]{3,2,1,0:T(8,128)(2,1)}, bf16[2,8,256,512]{3,2,1,0:T(8,128)(2,1)S(1)}, u32[]{:S(2)}) copy-start(bf16[2,8,256,512]{3,2,1,0:T(8,128)(2,1)S(1)} %divide_convert_fusion) | copy-start | bytes 12582916
  157.8 2.4 copy-start.3
  169.5 35.9 %collective-permute-start.3 = (bf16[256,8,128]{0,2,1:T(8,128)(2,1)}, bf16[256,8,128]{0,2,1:T(8,128)(2,1)}, u32[]{:S(2)}, u32[]{:S(2)}) collective-permute-start(bf16[256,8,128]{0,2,1:T(8,128)(2,1)} %fusion.58), channel_id=1, source_target_pairs={{0,30},{2,0},{4,2},{6,4},{8,6},{10,8},{12,10},{14,12},{16,14},{18,... | collective-permute-start | bytes 1572872 | tf_op jit(solution)/shard_map/ppermute | solution.py:14
  188.0 24.6 %collective-permute-start.2 = (bf16[256,8,128]{2,0,1:T(8,128)(2,1)}, bf16[256,8,128]{2,0,1:T(8,128)(2,1)}, u32[]{:S(2)}, u32[]{:S(2)}) collective-permute-start(bf16[256,8,128]{2,0,1:T(8,128)(2,1)} %fusion.57), channel_id=1, source_target_pairs={{0,30},{2,0},{4,2},{6,4},{8,6},{10,8},{12,10},{14,12},{16,14},{18,... | collective-permute-start | bytes 1572872 | tf_op jit(solution)/shard_map/ppermute | solution.py:14
  223.4 2.2 copy-start.8
  223.4 2.2 copy-start.9
  351.8 2.6 copy-start.4
  358.8 57.8 %copy-start.1 = (bf16[512,2048]{1,0:T(8,128)(2,1)S(1)}, bf16[512,2048]{1,0:T(8,128)(2,1)}, u32[]{:S(2)}) copy-start(bf16[512,2048]{1,0:T(8,128)(2,1)} %param.9) | copy-start | bytes 6291460
Sparse Core Ops, SparseCore 0:
  358.9 54.9 reduce-scatter.1
where the time goes:
time: 432 us; the launch traced here: 424 us
  waiting for transfers between devices  122 us (28%)
  blocking collectives  110 us (25%)
  matrix products  73.8 us (17%)
  local copies, waits for them, and re-layouts  49.7 us (12%)
  other arithmetic  27.2 us (6%)
  starting transfers between devices  26.9 us (6%)
  between operations  14.9 us (3%)
    all_to_all x1, blocking collectives, on_device(): lax.all_to_all(packed.reshape(devices, capacity, head_count, results.shap...  110 us
    reduce_scatter x1, waiting for transfers between devices, on_device(): lax.psum_scatter(partial_terms, 'head', scatter_dimension=1, tiled=True)  51.4 us
    all_to_all x1, waiting for transfers between devices, on_device(): lax.all_to_all(stacked, 'seq', split_axis=0, concat_axis=0, tiled=True)  47.6 us
    all_to_all x1, waiting for transfers between devices, on_device(): lax.all_to_all(grad_packed, 'seq', split_axis=0, concat_axis=0, tiled=True)  21.1 us
    all_to_all x1, starting transfers between devices, on_device(): lax.all_to_all(grad_packed, 'seq', split_axis=0, concat_axis=0, tiled=True)  15.5 us
    dot_general x1, matrix products, on_device(): jnp.einsum('nhqk,nqhd->nkhd', score_grad, query_blocks, preferred_element...  12.9 us
    dot_general x1, matrix products, on_device(): jnp.einsum('nhqk,nkhd->nqhd', score_grad, key_window, preferred_element_t...  12.3 us
    unnamed x28, local copies, waits for them, and re-layouts  12.2 us
  transfers between devices with their start and end apart: 7, of which 4 were waited for; matrix products, arithmetic and copies ran while one was open for 19% of the time, Pallas kernels for 0%

commit v1 on v0

v1 whole, which is shorter than its diff:
```python
import functools
import math

import jax
import jax.numpy as jnp
from jax import lax
from jax.experimental import pallas as pl
from jax.experimental.pallas import tpu as pltpu
from jax.sharding import PartitionSpec as P

GROUP = 256
NORM_EPS = 1e-06
MESH = pl.DeviceIdType.MESH
F32 = jnp.float32
BF16 = jnp.bfloat16


def slot_tables(sort_order, undo_order, tok_dev, capacity):
    target = undo_order // tok_dev
    same_target = target[:, :, None] == target[:, None, :]
    before = undo_order[:, None, :] < undo_order[:, :, None]
    outbound = target * capacity + jnp.sum((same_target & before).astype(jnp.int32), axis=2)
    source = sort_order // tok_dev
    same_source = source[:, :, None] == source[:, None, :]
    places = jnp.arange(tok_dev, dtype=jnp.int32)
    earlier = (places[None, :] < places[:, None])[None]
    inbound = source * capacity + jnp.sum((same_source & earlier).astype(jnp.int32), axis=2)
    return outbound, inbound


def dot(a, b, contract):
    return lax.dot_general(a, b, (contract, ((), ())), preferred_element_type=F32)


NN = ((1,), (0,))
NT = ((1,), (1,))
TN = ((0,), (0,))


def kernel(
    n, nh, capacity, head_size,
    qk_ref, v_ref, w_ref, og_ref, out_row, out_col, in_row, in_col,
    proj_ref, dqk_ref, dv_ref,
    send_x, send_g, send_o, recv_x, recv_g, recv_o, recv_d,
    sq, skv, halo, prob, acc_q, acc_k, acc_v, back_send, back,
    att, part_send, part_recv, own,
    sx, rx, sg, rg, so, ro, sd, rd, sh, rh, sb, rb, sp, rp,
):
    tok_dev, _ = qk_ref.shape
    heads = out_row.shape[0]
    slots = n * capacity
    step = math.gcd(slots, 256)
    blocks = tok_dev // GROUP
    scale = head_size ** (-0.5)
    me = lax.axis_index("seq")
    mh = lax.axis_index("head")
    after = lax.rem(me + 1, n)
    ahead = lax.rem(me + n - 1, n)

    barrier = pltpu.get_barrier_semaphore()

    def greet(d, _):
        pl.semaphore_signal(
            barrier, inc=1, device_id={"seq": lax.rem(me + d, n)}, device_id_type=MESH
        )
        return 0

    lax.fori_loop(1, n, greet, 0)
    for e in range(1, nh):
        pl.semaphore_signal(
            barrier, inc=1, device_id={"head": lax.rem(mh + e, nh)}, device_id_type=MESH
        )
    pl.semaphore_wait(barrier, n - 1 + nh - 1)

    def cols(h):
        return pl.ds(pl.multiple_of(h * head_size, head_size), head_size)

    def rows(b):
        return pl.ds(b * GROUP, GROUP)

    def spread(src, dst, h, send_sem, recv_sem):
        mine = pl.ds(pl.multiple_of(me * capacity, 16), capacity)

        def one(d, _):
            peer = lax.rem(me + d, n)
            pltpu.make_async_remote_copy(
                src_ref=src.at[h, pl.ds(pl.multiple_of(peer * capacity, 16), capacity)],
                dst_ref=dst.at[h, mine],
                send_sem=send_sem.at[h],
                recv_sem=recv_sem.at[h],
                device_id={"seq": peer},
                device_id_type=MESH,
            ).start()
            return 0

        lax.fori_loop(1, n, one, 0)
        pltpu.make_async_copy(src.at[h, mine], dst.at[h, mine], recv_sem.at[h]).start()

    def wait_all(ref, sem):
        pltpu.make_async_copy(ref, ref, sem).wait()

    def wait_sent(src, h, sem):
        wait_all(src.at[h, pl.ds(0, slots - capacity)], sem.at[h])

    def pack(row_table, h, values, dst):
        places = row_table[h]
        for c in range(slots // step):
            ids = lax.broadcasted_iota(jnp.int32, (step, tok_dev), 0) + c * step
            pick = jnp.where(ids == places, 1.0, 0.0).astype(BF16)
            dst[h, pl.ds(c * step, step), :] = dot(pick, values, NN).astype(BF16)

    def column(col_table, h, b):
        table = col_table[rows(b), :]
        lane = lax.broadcasted_iota(jnp.int32, table.shape, 1)
        return jnp.sum(jnp.where(lane == h, table, 0.0), axis=1, keepdims=True).astype(jnp.int32)

    def unpack(col_table, h, b, src):
        ids = lax.broadcasted_iota(jnp.int32, (GROUP, slots), 1)
        pick = jnp.where(ids == column(col_table, h, b), 1.0, 0.0).astype(BF16)
        return dot(pick, src[h], NN)

    def inverse_norm(q):
        return lax.rsqrt(jnp.mean(q * q, axis=1, keepdims=True) + NORM_EPS)

    def window(h, b):
        prior = halo[h] if b == 0 else skv[h, rows(b - 1), :]
        both = jnp.concatenate([prior, skv[h, rows(b), :]], axis=0)
        return both[:, :head_size], both[:, head_size:]

    def halo_copy(h):
        return pltpu.make_async_remote_copy(
            src_ref=skv.at[h, rows(blocks - 1)], dst_ref=halo.at[h],
            send_sem=sh.at[h], recv_sem=rh.at[h],
            device_id={"seq": after}, device_id_type=MESH,
        )

    def back_copy(h):
        return pltpu.make_async_remote_copy(
            src_ref=back_send.at[h], dst_ref=back.at[h],
            send_sem=sb.at[h], recv_sem=rb.at[h],
            device_id={"seq": ahead}, device_id_type=MESH,
        )

    def each_head(f):
        def go(h, _):
            f(h)
            return 0

        lax.fori_loop(0, heads, go, 0)

    def send_tokens(h):
        both = jnp.concatenate([qk_ref[:, cols(h)], v_ref[:, cols(h)]], axis=1)
        pack(out_row, h, both, send_x)
        spread(send_x, recv_x, h, sx, rx)

    def sort_tokens(h):
        wait_all(recv_x.at[h], rx.at[h])
        for b in range(blocks):
            arrived = unpack(in_col, h, b, recv_x)
            q = arrived[:, :head_size]
            sq[h, rows(b), :] = q.astype(BF16)
            skv[h, rows(b), :head_size] = (q * inverse_norm(q)).astype(BF16)
            skv[h, rows(b), head_size:] = arrived[:, head_size:].astype(BF16)
        halo_copy(h).start()
        grad = dot(og_ref[...], w_ref[cols(h), :], NT).astype(BF16)
        pack(out_row, h, grad, send_g)
        spread(send_g, recv_g, h, sg, rg)

    def forward(h):
        halo_copy(h).wait_recv()
        outs = []
        for b in range(blocks):
            keys, vals = window(h, b)
            scores = dot(sq[h, rows(b), :], keys, NT) * scale
            own_id = lax.broadcasted_iota(jnp.int32, scores.shape, 0) + GROUP
            other = lax.broadcasted_iota(jnp.int32, scores.shape, 1)
            weights = jnp.where(own_id != other, jnp.exp(scores), 0.0)
            probability = (weights / jnp.sum(weights, axis=1, keepdims=True)).astype(BF16)
            prob[h, rows(b), :] = probability
            outs.append(dot(probability, vals, NN).astype(BF16))
        pack(in_row, h, jnp.concatenate(outs, axis=0), send_o)
        spread(send_o, recv_o, h, so, ro)

    def backward(h):
        wait_all(recv_g.at[h], rg.at[h])
        for b in range(blocks):
            keys, vals = window(h, b)
            grad = unpack(in_col, h, b, recv_g).astype(BF16)
            probability = prob[h, rows(b), :]
            wide = probability.astype(F32)
            prob_grad = dot(grad, vals, NT)
            delta = jnp.sum(wide * prob_grad, axis=1, keepdims=True)
            score_grad = (wide * (prob_grad - delta) * scale).astype(BF16)
            acc_q[h, rows(b), :] = dot(score_grad, keys, NN)
            v_part = dot(probability, grad, TN)
            k_part = dot(score_grad, sq[h, rows(b), :], TN)
            if b == 0:
                back_send[h, :, :head_size] = k_part[:GROUP].astype(BF16)
                back_send[h, :, head_size:] = v_part[:GROUP].astype(BF16)
                back_copy(h).start()
            else:
                acc_k[h, rows(b - 1), :] += k_part[:GROUP]
                acc_v[h, rows(b - 1), :] += v_part[:GROUP]
            acc_k[h, rows(b), :] = k_part[GROUP:]
            acc_v[h, rows(b), :] = v_part[GROUP:]

    def finish(h):
        back_copy(h).wait_recv()
        wait_sent(send_x, h, sx)
        done = []
        for b in range(blocks):
            k_grad = acc_k[h, rows(b), :]
            v_grad = acc_v[h, rows(b), :]
            if b == blocks - 1:
                k_grad += back[h, :, :head_size].astype(F32)
                v_grad += back[h, :, head_size:].astype(F32)
            q = sq[h, rows(b), :].astype(F32)
            norm = inverse_norm(q)
            inner = jnp.sum(k_grad * q, axis=1, keepdims=True) / head_size
            shared = acc_q[h, rows(b), :] + norm * k_grad - norm * norm * norm * inner * q
            done.append(jnp.concatenate([shared.astype(BF16), v_grad.astype(BF16)], axis=1))
        pack(in_row, h, jnp.concatenate(done, axis=0), send_x)
        spread(send_x, recv_d, h, sd, rd)

    def collect_out(h):
        wait_all(recv_o.at[h], ro.at[h])
        for b in range(blocks):
            att[rows(b), cols(h)] = unpack(out_col, h, b, recv_o).astype(BF16)

    def collect_grads(h):
        wait_all(recv_d.at[h], rd.at[h])
        for b in range(blocks):
            arrived = unpack(out_col, h, b, recv_d).astype(BF16)
            dqk_ref[rows(b), cols(h)] = arrived[:, :head_size]
            dv_ref[rows(b), cols(h)] = arrived[:, head_size:]

    each_head(send_tokens)
    each_head(sort_tokens)
    each_head(forward)
    each_head(backward)
    each_head(finish)
    each_head(collect_out)

    width = proj_ref.shape[1]
    tile = math.gcd(width, 256)

    def project(owner, write):
        def go(c, _):
            at = pl.multiple_of(c * tile, tile)
            taken = pl.ds(pl.multiple_of(owner * width + c * tile, tile), tile)
            write(pl.ds(at, tile), dot(att[...], w_ref[:, taken], NN))
            return 0

        lax.fori_loop(0, width // tile, go, 0)

    def part_copy(e):
        return pltpu.make_async_remote_copy(
            src_ref=part_send.at[e - 1], dst_ref=part_recv.at[e - 1],
            send_sem=sp.at[e - 1], recv_sem=rp.at[e - 1],
            device_id={"head": lax.rem(mh + e, nh)}, device_id_type=MESH,
        )

    for e in range(1, nh):
        def write_part(at, part, e=e):
            part_send[e - 1, :, at] = part.astype(BF16)

        project(lax.rem(mh + e, nh), write_part)
        part_copy(e).start()

    def write_own(at, part):
        own[:, at] = part

    project(mh, write_own)
    each_head(collect_grads)
    for e in range(1, nh):
        part_copy(e).wait_recv()
        own[...] += part_recv[e - 1].astype(F32)
    proj_ref[...] = own[...].astype(BF16)

    def drain(h):
        wait_sent(send_x, h, sd)
        wait_sent(send_g, h, sg)
        wait_sent(send_o, h, so)
        halo_copy(h).wait_send()
        back_copy(h).wait_send()

    each_head(drain)
    for e in range(1, nh):
        part_copy(e).wait_send()


def on_device(query_key, values, out_weight, out_grad, sort_order, undo_order):
    tok_dev, flat_width = query_key.shape
    heads = sort_order.shape[0]
    head_size = flat_width // heads
    n = lax.axis_size("seq")
    nh = lax.axis_size("head")
    most = 3 * tok_dev // (2 * n)
    capacity = (most + 15) // 16 * 16
    slots = n * capacity
    width = out_weight.shape[1] // nh
    outbound, inbound = slot_tables(sort_order, undo_order, tok_dev, capacity)
    vmem = pl.BlockSpec(memory_space=pltpu.VMEM)
    sems = pltpu.SemaphoreType.DMA((heads,))
    shape = jax.ShapeDtypeStruct
    return pl.pallas_call(
        functools.partial(kernel, n, nh, capacity, head_size),
        out_shape=(
            shape((tok_dev, width), BF16),
            shape((tok_dev, flat_width), BF16),
            shape((tok_dev, flat_width), BF16),
        ),
        in_specs=[vmem] * 8,
        out_specs=(vmem, vmem, vmem),
        scratch_shapes=[
            pltpu.VMEM((heads, slots, 2 * head_size), BF16),
            pltpu.VMEM((heads, slots, head_size), BF16),
            pltpu.VMEM((heads, slots, head_size), BF16),
            pltpu.VMEM((heads, slots, 2 * head_size), BF16),
            pltpu.VMEM((heads, slots, head_size), BF16),
            pltpu.VMEM((heads, slots, head_size), BF16),
            pltpu.VMEM((heads, slots, 2 * head_size), BF16),
            pltpu.VMEM((heads, tok_dev, head_size), BF16),
            pltpu.VMEM((heads, tok_dev, 2 * head_size), BF16),
            pltpu.VMEM((heads, GROUP, 2 * head_size), BF16),
            pltpu.VMEM((heads, tok_dev, 2 * GROUP), BF16),
            pltpu.VMEM((heads, tok_dev, head_size), F32),
            pltpu.VMEM((heads, tok_dev, head_size), F32),
            pltpu.VMEM((heads, tok_dev, head_size), F32),
            pltpu.VMEM((heads, GROUP, 2 * head_size), BF16),
            pltpu.VMEM((heads, GROUP, 2 * head_size), BF16),
            pltpu.VMEM((tok_dev, flat_width), BF16),
            pltpu.VMEM((max(nh - 1, 1), tok_dev, width), BF16),
            pltpu.VMEM((max(nh - 1, 1), tok_dev, width), BF16),
            pltpu.VMEM((tok_dev, width), F32),
        ]
        + [sems] * 12
        + [pltpu.SemaphoreType.DMA((max(nh - 1, 1),))] * 2,
        compiler_params=pltpu.CompilerParams(
            collective_id=0, has_side_effects=True, vmem_limit_bytes=62 * 2**20
        ),
        cost_estimate=pl.CostEstimate(
            flops=2 * 10**10, bytes_accessed=2**24, transcendentals=2**21
        ),
    )(
        query_key, values, out_weight, out_grad,
        outbound[:, None, :], outbound.T.astype(F32),
        inbound[:, None, :], inbound.T.astype(F32),
    )


def solution(mesh):
    placed = (
        P("seq", "head"),
        P("seq", "head"),
        P("head", None),
        P("seq", None),
        P("head", "seq"),
        P("head", "seq"),
    )
    return jax.shard_map(
        on_device,
        mesh=mesh,
        in_specs=placed,
        out_specs=(P("seq", "head"), P("seq", "head"), P("seq", "head")),
        check_vma=False,
    )
```

time: 432 us -> 252 us (0.58)
  the two profiles are of different devices: /device:TPU:0 before, /device:TPU:29 now
where the time goes in v1:
time: 252 us; the launch traced here: 251 us
  Pallas kernels  235 us (93%)
  local copies, waits for them, and re-layouts  9.1 us (4%)
  other arithmetic  6.66 us (3%)
    pallas_call x1, Pallas kernels, on_device(): pl.pallas_call(functools.partial(kernel, n, nh, capacity, head_size), out...  235 us
    unnamed x7, local copies, waits for them, and re-layouts  7.27 us

profile of v1, /device:TPU:29, one launch (start us, length us, event | category | flops | bytes accessed | tf_op | source)
XLA Modules:
  0.0 251.2 jit_solution(1407109643260631025)
XLA Ops:
  0.6 0.8 copy.30
  1.5 0.8 copy.23
  2.3 0.1 add_select_fusion.1
  2.5 0.1 copy.27
  2.6 2.9 %convert_reduce_fusion.1 = s32[8,512]{1,0:T(8,128)S(1)} fusion(s32[8,512]{1,0:T(8,128)} %param.11, s32[8,512]{1,0:T(8,128)S(1)} %copy.27), kind=kLoop, calls=%fused_computation.1 | loop fusion | flops 10481664 | bytes 49152 | tf_op jit(solution)/shard_map/reduce_sum | solution.py:22
  5.5 0.1 copy.29
  5.6 0.1 add_select_fusion
  5.8 0.1 copy.34
  5.9 0.1 iota_compare_fusion
  6.0 2.2 convert_reduce_fusion
  8.2 0.1 copy.36
  8.3 1.1 convert_bitcast_fusion
  9.5 0.7 copy.38.in_row
  10.2 0.7 copy.37.out_row
  10.9 234.7 %shard_map.85 = (bf16[512,1024]{1,0:T(8,128)(2,1)}, bf16[512,1024]{1,0:T(8,128)(2,1)}, bf16[512,1024]{1,0:T(8,128)(2,1)}) custom-call(bf16[512,1024]{1,0:T(8,128)(2,1)} %qk_ref.1, bf16[512,1024]{1,0:T(8,128)(2,1)} %v_ref.1, bf16[1024,2048]{1,0:T(8,128)(2,1)} %w_ref.1, bf16[512,2048]{1,0:T(8,128)(2,1)} %og_ref.1, s32[8,1,512]{2,1,0:T(1,128)} %copy.37.out_row, ...), custom_call_target="tpu_custom_call" | custom-call | flops 20000000000 | bytes 16777216 | tf_op jit(solution)/shard_map/pallas_call | solution.py:306
  245.6 0.0 copy-start
  245.6 2.4 copy.42
  247.9 2.3 copy.43
  250.2 0.0 copy-done
  250.2 1.0 copy.44
Async XLA Ops:
  245.6 4.6 %copy-start = (bf16[512,1024]{1,0:T(8,128)(2,1)S(1)}, bf16[512,1024]{1,0:T(8,128)(2,1)}, u32[]{:S(2)}) copy-start(bf16[512,1024]{1,0:T(8,128)(2,1)} %get-tuple-element.14) | copy-start | bytes 3145732

commit v2 on v1

--- a/solution.py
+++ b/solution.py
@@ -15,17 +15,8 @@
 BF16 = jnp.bfloat16
 
 
-def slot_tables(sort_order, undo_order, tok_dev, capacity):
-    target = undo_order // tok_dev
-    same_target = target[:, :, None] == target[:, None, :]
-    before = undo_order[:, None, :] < undo_order[:, :, None]
-    outbound = target * capacity + jnp.sum((same_target & before).astype(jnp.int32), axis=2)
-    source = sort_order // tok_dev
-    same_source = source[:, :, None] == source[:, None, :]
-    places = jnp.arange(tok_dev, dtype=jnp.int32)
-    earlier = (places[None, :] < places[:, None])[None]
-    inbound = source * capacity + jnp.sum((same_source & earlier).astype(jnp.int32), axis=2)
-    return outbound, inbound
+def quotient(x, by):
+    return x >> (by.bit_length() - 1) if by & (by - 1) == 0 else lax.div(x, jnp.int32(by))
 
 
 def dot(a, b, contract):
@@ -39,12 +30,14 @@
 
 def kernel(
     n, nh, capacity, head_size,
-    qk_ref, v_ref, w_ref, og_ref, out_row, out_col, in_row, in_col,
-    proj_ref, dqk_ref, dv_ref,
+    qk_hbm, v_hbm, w_hbm, og_hbm, sort_ref, undo_ref,
+    proj_out, dqk_out, dv_out,
+    qk_ref, v_ref, w_ref, og_ref, proj_ref, dqk_ref, dv_ref,
+    out_row, out_col, in_row, in_col,
     send_x, send_g, send_o, recv_x, recv_g, recv_o, recv_d,
-    sq, skv, halo, prob, acc_q, acc_k, acc_v, back_send, back,
+    sq, skv, halo, acc_q, acc_k, acc_v, back_send, back,
     att, part_send, part_recv, own,
-    sx, rx, sg, rg, so, ro, sd, rd, sh, rh, sb, rb, sp, rp,
+    sx, rx, sg, rg, so, ro, sd, rd, sh, rh, sb, rb, oq, ov, sp, rp, load, op,
 ):
     tok_dev, _ = qk_ref.shape
     heads = out_row.shape[0]
@@ -70,7 +63,16 @@
         pl.semaphore_signal(
             barrier, inc=1, device_id={"head": lax.rem(mh + e, nh)}, device_id_type=MESH
         )
-    pl.semaphore_wait(barrier, n - 1 + nh - 1)
+    loads = [
+        pltpu.make_async_copy(src, dst, load.at[i])
+        for i, (src, dst) in enumerate(
+            [(qk_hbm, qk_ref), (v_hbm, v_ref), (w_hbm, w_ref), (og_hbm, og_ref)]
+        )
+    ]
+    for copy in loads:
+        copy.start()
+    out_col[...] = jnp.zeros_like(out_col)
+    in_col[...] = jnp.zeros_like(in_col)
 
     def cols(h):
         return pl.ds(pl.multiple_of(h * head_size, head_size), head_size)
@@ -109,6 +111,47 @@
             pick = jnp.where(ids == places, 1.0, 0.0).astype(BF16)
             dst[h, pl.ds(c * step, step), :] = dot(pick, values, NN).astype(BF16)
 
+    square = (tok_dev, tok_dev)
+
+    def down():
+        return lax.broadcasted_iota(jnp.int32, square, 0)
+
+    def across():
+        return lax.broadcasted_iota(jnp.int32, square, 1)
+
+    def count(mask, axis):
+        return jnp.sum(jnp.where(mask, 1.0, 0.0), axis=axis, keepdims=True)
+
+    def as_column(row):
+        picked = jnp.where(down() == across(), row.astype(F32), 0.0)
+        return jnp.sum(picked, axis=1, keepdims=True).astype(jnp.int32)
+
+    def put(row_table, col_table, h, row, col):
+        row_table[h] = row.astype(jnp.int32)
+        lane = lax.broadcasted_iota(jnp.int32, col_table.shape, 1)
+        col_table[...] = jnp.where(lane == h, col, col_table[...])
+
+    def send_slots(h):
+        row = undo_ref[pl.ds(h, 1), :]
+        col = as_column(row)
+        to_row, to_col = quotient(row, tok_dev), quotient(col, tok_dev)
+        same = to_row == to_col
+        put(
+            out_row, out_col, h,
+            (to_row * capacity).astype(F32) + count(same & (col < row), 0),
+            (to_col * capacity).astype(F32) + count(same & (row < col), 1),
+        )
+
+    def arrival_slots(h):
+        row = quotient(sort_ref[pl.ds(h, 1), :], tok_dev)
+        col = as_column(row)
+        same = row == col
+        put(
+            in_row, in_col, h,
+            (row * capacity).astype(F32) + count(same & (down() < across()), 0),
+            (col * capacity).astype(F32) + count(same & (across() < down()), 1),
+        )
+
     def column(col_table, h, b):
         table = col_table[rows(b), :]
         lane = lax.broadcasted_iota(jnp.int32, table.shape, 1)
@@ -141,19 +184,24 @@
             device_id={"seq": ahead}, device_id_type=MESH,
         )
 
-    def each_head(f):
+    def each_head(f, first=0, last=heads):
         def go(h, _):
             f(h)
             return 0
 
-        lax.fori_loop(0, heads, go, 0)
-
-    def send_tokens(h):
+        lax.fori_loop(first, last, go, 0)
+
+    def pack_tokens(h):
         both = jnp.concatenate([qk_ref[:, cols(h)], v_ref[:, cols(h)]], axis=1)
         pack(out_row, h, both, send_x)
+
+    def send_tokens(h):
+        send_slots(h)
+        pack_tokens(h)
         spread(send_x, recv_x, h, sx, rx)
 
     def sort_tokens(h):
+        arrival_slots(h)
         wait_all(recv_x.at[h], rx.at[h])
         for b in range(blocks):
             arrived = unpack(in_col, h, b, recv_x)
@@ -166,34 +214,27 @@
         pack(out_row, h, grad, send_g)
         spread(send_g, recv_g, h, sg, rg)
 
-    def forward(h):
+    def attend(h):
         halo_copy(h).wait_recv()
+        wait_all(recv_g.at[h], rg.at[h])
         outs = []
         for b in range(blocks):
             keys, vals = window(h, b)
-            scores = dot(sq[h, rows(b), :], keys, NT) * scale
+            q = sq[h, rows(b), :]
+            scores = dot(q, keys, NT) * scale
             own_id = lax.broadcasted_iota(jnp.int32, scores.shape, 0) + GROUP
             other = lax.broadcasted_iota(jnp.int32, scores.shape, 1)
             weights = jnp.where(own_id != other, jnp.exp(scores), 0.0)
             probability = (weights / jnp.sum(weights, axis=1, keepdims=True)).astype(BF16)
-            prob[h, rows(b), :] = probability
             outs.append(dot(probability, vals, NN).astype(BF16))
-        pack(in_row, h, jnp.concatenate(outs, axis=0), send_o)
-        spread(send_o, recv_o, h, so, ro)
-
-    def backward(h):
-        wait_all(recv_g.at[h], rg.at[h])
-        for b in range(blocks):
-            keys, vals = window(h, b)
             grad = unpack(in_col, h, b, recv_g).astype(BF16)
-            probability = prob[h, rows(b), :]
             wide = probability.astype(F32)
             prob_grad = dot(grad, vals, NT)
             delta = jnp.sum(wide * prob_grad, axis=1, keepdims=True)
             score_grad = (wide * (prob_grad - delta) * scale).astype(BF16)
             acc_q[h, rows(b), :] = dot(score_grad, keys, NN)
             v_part = dot(probability, grad, TN)
-            k_part = dot(score_grad, sq[h, rows(b), :], TN)
+            k_part = dot(score_grad, q, TN)
             if b == 0:
                 back_send[h, :, :head_size] = k_part[:GROUP].astype(BF16)
                 back_send[h, :, head_size:] = v_part[:GROUP].astype(BF16)
@@ -203,6 +244,8 @@
                 acc_v[h, rows(b - 1), :] += v_part[:GROUP]
             acc_k[h, rows(b), :] = k_part[GROUP:]
             acc_v[h, rows(b), :] = v_part[GROUP:]
+        pack(in_row, h, jnp.concatenate(outs, axis=0), send_o)
+        spread(send_o, recv_o, h, so, ro)
 
     def finish(h):
         back_copy(h).wait_recv()
@@ -233,12 +276,35 @@
             arrived = unpack(out_col, h, b, recv_d).astype(BF16)
             dqk_ref[rows(b), cols(h)] = arrived[:, :head_size]
             dv_ref[rows(b), cols(h)] = arrived[:, head_size:]
-
-    each_head(send_tokens)
+        for copy in grad_copies(h):
+            copy.start()
+
+    def grad_copies(h):
+        at = (slice(None), cols(h))
+        return (
+            pltpu.make_async_copy(dqk_ref.at[at], dqk_out.at[at], oq.at[h]),
+            pltpu.make_async_copy(dv_ref.at[at], dv_out.at[at], ov.at[h]),
+        )
+
+    send_slots(0)
+    loads[0].wait()
+    loads[1].wait()
+    pack_tokens(0)
+    pl.semaphore_wait(barrier, n - 1 + nh - 1)
+    spread(send_x, recv_x, 0, sx, rx)
+    each_head(send_tokens, 1)
+    loads[2].wait()
+    loads[3].wait()
     each_head(sort_tokens)
-    each_head(forward)
-    each_head(backward)
-    each_head(finish)
+    lag = heads // 2
+
+    def attend_and_finish(h):
+        attend(h)
+        finish(h - lag)
+
+    each_head(attend, 0, lag)
+    each_head(attend_and_finish, lag)
+    each_head(finish, heads - lag)
     each_head(collect_out)
 
     width = proj_ref.shape[1]
@@ -271,13 +337,18 @@
         own[:, at] = part
 
     project(mh, write_own)
-    each_head(collect_grads)
+    each_head(collect_grads, 0, heads - 1)
     for e in range(1, nh):
         part_copy(e).wait_recv()
         own[...] += part_recv[e - 1].astype(F32)
     proj_ref[...] = own[...].astype(BF16)
+    proj_copy = pltpu.make_async_copy(proj_ref, proj_out, op.at[0])
+    proj_copy.start()
+    collect_grads(heads - 1)
 
     def drain(h):
+        for copy in grad_copies(h):
+            copy.wait()
         wait_sent(send_x, h, sd)
         wait_sent(send_g, h, sg)
         wait_sent(send_o, h, so)
@@ -287,6 +358,26 @@
     each_head(drain)
     for e in range(1, nh):
         part_copy(e).wait_send()
+    proj_copy.wait()
+
+
+def hand_over(parts, *refs):
+    count = (len(refs) - 1) // 2
+    sems = refs[-1]
+    copies = []
+    for i in range(count):
+        length = refs[i].shape[0] // parts
+        for c in range(parts):
+            at = pl.ds(c * length, length)
+            copies.append(
+                pltpu.make_async_copy(
+                    refs[i].at[at], refs[count + i].at[at], sems.at[i * parts + c]
+                )
+            )
+    for copy in copies:
+        copy.start()
+    for copy in copies:
+        copy.wait()
 
 
 def on_device(query_key, values, out_weight, out_grad, sort_order, undo_order):
@@ -299,20 +390,31 @@
     capacity = (most + 15) // 16 * 16
     slots = n * capacity
     width = out_weight.shape[1] // nh
-    outbound, inbound = slot_tables(sort_order, undo_order, tok_dev, capacity)
     vmem = pl.BlockSpec(memory_space=pltpu.VMEM)
     sems = pltpu.SemaphoreType.DMA((heads,))
+    anywhere = pl.BlockSpec(memory_space=pl.ANY)
     shape = jax.ShapeDtypeStruct
-    return pl.pallas_call(
+    results = pl.pallas_call(
         functools.partial(kernel, n, nh, capacity, head_size),
         out_shape=(
             shape((tok_dev, width), BF16),
             shape((tok_dev, flat_width), BF16),
             shape((tok_dev, flat_width), BF16),
         ),
-        in_specs=[vmem] * 8,
-        out_specs=(vmem, vmem, vmem),
+        in_specs=[anywhere] * 4 + [vmem] * 2,
+        out_specs=(anywhere,) * 3,
         scratch_shapes=[
+            pltpu.VMEM(query_key.shape, BF16),
+            pltpu.VMEM(values.shape, BF16),
+            pltpu.VMEM(out_weight.shape, BF16),
+            pltpu.VMEM(out_grad.shape, BF16),
+            pltpu.VMEM((tok_dev, width), BF16),
+            pltpu.VMEM((tok_dev, flat_width), BF16),
+            pltpu.VMEM((tok_dev, flat_width), BF16),
+            pltpu.VMEM((heads, 1, tok_dev), jnp.int32),
+            pltpu.VMEM((tok_dev, heads), F32),
+            pltpu.VMEM((heads, 1, tok_dev), jnp.int32),
+            pltpu.VMEM((tok_dev, heads), F32),
             pltpu.VMEM((heads, slots, 2 * head_size), BF16),
             pltpu.VMEM((heads, slots, head_size), BF16),
             pltpu.VMEM((heads, slots, head_size), BF16),
@@ -323,7 +425,6 @@
             pltpu.VMEM((heads, tok_dev, head_size), BF16),
             pltpu.VMEM((heads, tok_dev, 2 * head_size), BF16),
             pltpu.VMEM((heads, GROUP, 2 * head_size), BF16),
-            pltpu.VMEM((heads, tok_dev, 2 * GROUP), BF16),
             pltpu.VMEM((heads, tok_dev, head_size), F32),
             pltpu.VMEM((heads, tok_dev, head_size), F32),
             pltpu.VMEM((heads, tok_dev, head_size), F32),
@@ -334,8 +435,9 @@
             pltpu.VMEM((max(nh - 1, 1), tok_dev, width), BF16),
             pltpu.VMEM((tok_dev, width), F32),
         ]
-        + [sems] * 12
-        + [pltpu.SemaphoreType.DMA((max(nh - 1, 1),))] * 2,
+        + [sems] * 14
+        + [pltpu.SemaphoreType.DMA((max(nh - 1, 1),))] * 2
+        + [pltpu.SemaphoreType.DMA((4,)), pltpu.SemaphoreType.DMA((1,))],
         compiler_params=pltpu.CompilerParams(
             collective_id=0, has_side_effects=True, vmem_limit_bytes=62 * 2**20
         ),
@@ -343,10 +445,19 @@
             flops=2 * 10**10, bytes_accessed=2**24, transcendentals=2**21
         ),
     )(
-        query_key, values, out_weight, out_grad,
-        outbound[:, None, :], outbound.T.astype(F32),
-        inbound[:, None, :], inbound.T.astype(F32),
+        query_key, values, out_weight, out_grad, sort_order, undo_order
     )
+    parts = 4
+    return pl.pallas_call(
+        functools.partial(hand_over, parts),
+        out_shape=tuple(shape(r.shape, r.dtype) for r in results),
+        in_specs=[anywhere] * 3,
+        out_specs=(anywhere,) * 3,
+        scratch_shapes=[pltpu.SemaphoreType.DMA((3 * parts,))],
+        cost_estimate=pl.CostEstimate(
+            flops=0, bytes_accessed=6 * values.size * 2, transcendentals=0
+        ),
+    )(*results)
 
 
 def solution(mesh):

time: 252 us -> 338 us (1.34)
  the two profiles are of different devices: /device:TPU:29 before, /device:TPU:0 now
where the time goes in v2:
time: 338 us
  Pallas kernels  337 us (100%)
    pallas_call x1, Pallas kernels, on_device(): pl.pallas_call(functools.partial(kernel, n, nh, capacity, head_size), out...  241 us
    pallas_call x1, Pallas kernels, on_device(): pl.pallas_call(functools.partial(hand_over, parts), out_shape=tuple((shap...  96.5 us

profile of v2, /device:TPU:0, one launch (start us, length us, event | category | flops | bytes accessed | tf_op | source)
XLA Modules:
  0.0 337.7 jit_solution(16589563213341586745)
XLA Ops:
  0.6 240.6 %shard_map.85 = (bf16[512,1024]{1,0:T(8,128)(2,1)}, bf16[512,1024]{1,0:T(8,128)(2,1)}, bf16[512,1024]{1,0:T(8,128)(2,1)}) custom-call(bf16[512,1024]{1,0:T(8,128)(2,1)} %qk_hbm.1, bf16[512,1024]{1,0:T(8,128)(2,1)} %v_hbm.1, bf16[1024,2048]{1,0:T(8,128)(2,1)} %w_hbm.1, bf16[512,2048]{1,0:T(8,128)(2,1)} %og_hbm.1, s32[8,512]{1,0:T(8,128)} %sort_ref.1, ...), custom_call_target="tpu_custom_call" | custom-call | flops 20000000000 | bytes 16777216 | tf_op jit(solution)/shard_map/pallas_call | solution.py:397
  241.2 96.5 %shard_map.86 = (bf16[512,1024]{1,0:T(8,128)(2,1)}, bf16[512,1024]{1,0:T(8,128)(2,1)}, bf16[512,1024]{1,0:T(8,128)(2,1)}) custom-call(bf16[512,1024]{1,0:T(8,128)(2,1)} %get-tuple-element.6.refs_0_, bf16[512,1024]{1,0:T(8,128)(2,1)} %get-tuple-element.7.refs_1_, bf16[512,1024]{1,0:T(8,128)(2,1)} %get-tuple-element.8.refs_2_), custom_call_target="tpu_custom_call" | custom-call | bytes 6291456 | tf_op jit(solution)/shard_map/pallas_call | solution.py:451

commit v3 on v2

--- a/solution.py
+++ b/solution.py
@@ -83,8 +83,8 @@
     def spread(src, dst, h, send_sem, recv_sem):
         mine = pl.ds(pl.multiple_of(me * capacity, 16), capacity)
 
-        def one(d, _):
-            peer = lax.rem(me + d, n)
+        def one(i, _):
+            peer = lax.rem(me + i // 2 + (i % 2) * (n // 2), n)
             pltpu.make_async_remote_copy(
                 src_ref=src.at[h, pl.ds(pl.multiple_of(peer * capacity, 16), capacity)],
                 dst_ref=dst.at[h, mine],
@@ -296,15 +296,9 @@
     loads[2].wait()
     loads[3].wait()
     each_head(sort_tokens)
-    lag = heads // 2
-
-    def attend_and_finish(h):
-        attend(h)
-        finish(h - lag)
-
-    each_head(attend, 0, lag)
-    each_head(attend_and_finish, lag)
-    each_head(finish, heads - lag)
+    early = heads // 2
+    each_head(attend)
+    each_head(finish, 0, early)
     each_head(collect_out)
 
     width = proj_ref.shape[1]
@@ -332,6 +326,8 @@
 
         project(lax.rem(mh + e, nh), write_part)
         part_copy(e).start()
+
+    each_head(finish, early)
 
     def write_own(at, part):
         own[:, at] = part
@@ -361,23 +357,10 @@
     proj_copy.wait()
 
 
-def hand_over(parts, *refs):
-    count = (len(refs) - 1) // 2
-    sems = refs[-1]
-    copies = []
-    for i in range(count):
-        length = refs[i].shape[0] // parts
-        for c in range(parts):
-            at = pl.ds(c * length, length)
-            copies.append(
-                pltpu.make_async_copy(
-                    refs[i].at[at], refs[count + i].at[at], sems.at[i * parts + c]
-                )
-            )
-    for copy in copies:
-        copy.start()
-    for copy in copies:
-        copy.wait()
+def hand_over(*refs):
+    half = len(refs) // 2
+    for source, target in zip(refs[:half], refs[half:]):
+        target[...] = source[...]
 
 
 def on_device(query_key, values, out_weight, out_grad, sort_order, undo_order):
@@ -447,13 +430,17 @@
     )(
         query_key, values, out_weight, out_grad, sort_order, undo_order
     )
-    parts = 4
+    steps = 4
+
+    def slab(r):
+        return pl.BlockSpec((tok_dev // steps, r.shape[1]), lambda i: (i, 0))
+
     return pl.pallas_call(
-        functools.partial(hand_over, parts),
+        hand_over,
+        grid=(steps,),
         out_shape=tuple(shape(r.shape, r.dtype) for r in results),
-        in_specs=[anywhere] * 3,
-        out_specs=(anywhere,) * 3,
-        scratch_shapes=[pltpu.SemaphoreType.DMA((3 * parts,))],
+        in_specs=[slab(r) for r in results],
+        out_specs=tuple(slab(r) for r in results),
         cost_estimate=pl.CostEstimate(
             flops=0, bytes_accessed=6 * values.size * 2, transcendentals=0
         ),

time: 338 us -> 236 us (0.70)
  the two profiles are of different devices: /device:TPU:0 before, /device:TPU:21 now
where the time goes in v3:
time: 236 us
  Pallas kernels  235 us (100%)
    pallas_call x1, Pallas kernels, on_device(): pl.pallas_call(functools.partial(kernel, n, nh, capacity, head_size), out...  231 us

profile of v3, /device:TPU:21, one launch (start us, length us, event | category | flops | bytes accessed | tf_op | source)
XLA Modules:
  0.0 235.9 jit_solution(7686307057777020995)
XLA Ops:
  0.6 231.1 %shard_map.85 = (bf16[512,1024]{1,0:T(8,128)(2,1)}, bf16[512,1024]{1,0:T(8,128)(2,1)}, bf16[512,1024]{1,0:T(8,128)(2,1)}) custom-call(bf16[512,1024]{1,0:T(8,128)(2,1)} %qk_hbm.1, bf16[512,1024]{1,0:T(8,128)(2,1)} %v_hbm.1, bf16[1024,2048]{1,0:T(8,128)(2,1)} %w_hbm.1, bf16[512,2048]{1,0:T(8,128)(2,1)} %og_hbm.1, s32[8,512]{1,0:T(8,128)} %sort_ref.1, ...), custom_call_target="tpu_custom_call" | custom-call | flops 20000000000 | bytes 16777216 | tf_op jit(solution)/shard_map/pallas_call | solution.py:380
  231.7 4.1 %shard_map.86 = (bf16[512,1024]{1,0:T(8,128)(2,1)}, bf16[512,1024]{1,0:T(8,128)(2,1)}, bf16[512,1024]{1,0:T(8,128)(2,1)}) custom-call(bf16[512,1024]{1,0:T(8,128)(2,1)} %get-tuple-element.6.refs_0_, bf16[512,1024]{1,0:T(8,128)(2,1)} %get-tuple-element.7.refs_1_, bf16[512,1024]{1,0:T(8,128)(2,1)} %get-tuple-element.8.refs_2_), custom_call_target="tpu_custom_call" | custom-call | bytes 6291456 | tf_op jit(solution)/shard_map/pallas_call | solution.py:438

commit v4 on v3

--- a/solution.py
+++ b/solution.py
@@ -69,7 +69,7 @@
             [(qk_hbm, qk_ref), (v_hbm, v_ref), (w_hbm, w_ref), (og_hbm, og_ref)]
         )
     ]
-    for copy in loads:
+    for copy in loads[:2]:
         copy.start()
     out_col[...] = jnp.zeros_like(out_col)
     in_col[...] = jnp.zeros_like(in_col)
@@ -225,7 +225,7 @@
             own_id = lax.broadcasted_iota(jnp.int32, scores.shape, 0) + GROUP
             other = lax.broadcasted_iota(jnp.int32, scores.shape, 1)
             weights = jnp.where(own_id != other, jnp.exp(scores), 0.0)
-            probability = (weights / jnp.sum(weights, axis=1, keepdims=True)).astype(BF16)
+            probability = (weights * (1.0 / jnp.sum(weights, axis=1, keepdims=True))).astype(BF16)
             outs.append(dot(probability, vals, NN).astype(BF16))
             grad = unpack(in_col, h, b, recv_g).astype(BF16)
             wide = probability.astype(F32)
@@ -289,15 +289,28 @@
     send_slots(0)
     loads[0].wait()
     loads[1].wait()
+    for copy in loads[2:]:
+        copy.start()
     pack_tokens(0)
     pl.semaphore_wait(barrier, n - 1 + nh - 1)
     spread(send_x, recv_x, 0, sx, rx)
-    each_head(send_tokens, 1)
+    early = heads // 2
+    late = heads - early
+
+    def send_and_sort(h):
+        send_tokens(h + early)
+        sort_tokens(h)
+
+    def sort_and_attend(h):
+        sort_tokens(h)
+        attend(h - late)
+
+    each_head(send_tokens, 1, early)
     loads[2].wait()
     loads[3].wait()
-    each_head(sort_tokens)
-    early = heads // 2
-    each_head(attend)
+    each_head(send_and_sort, 0, late)
+    each_head(sort_and_attend, late)
+    each_head(attend, early)
     each_head(finish, 0, early)
     each_head(collect_out)
 
@@ -357,10 +370,25 @@
     proj_copy.wait()
 
 
-def hand_over(*refs):
-    half = len(refs) // 2
-    for source, target in zip(refs[:half], refs[half:]):
-        target[...] = source[...]
+def hand_over(steps, *refs):
+    *refs, loaded, stored = refs
+    count = len(refs) // 3
+    loads, stores = [], []
+    for i in range(count):
+        source, target, held = refs[i], refs[count + i], refs[2 * count + i]
+        length = source.shape[0] // steps
+        for c in range(steps):
+            at = pl.ds(c * length, length)
+            own = i * steps + c
+            loads.append(pltpu.make_async_copy(source.at[at], held.at[at], loaded.at[own]))
+            stores.append(pltpu.make_async_copy(held.at[at], target.at[at], stored.at[own]))
+    for load in loads:
+        load.start()
+    for load, store in zip(loads, stores):
+        load.wait()
+        store.start()
+    for store in stores:
+        store.wait()
 
 
 def on_device(query_key, values, out_weight, out_grad, sort_order, undo_order):
@@ -431,16 +459,14 @@
         query_key, values, out_weight, out_grad, sort_order, undo_order
     )
     steps = 4
-
-    def slab(r):
-        return pl.BlockSpec((tok_dev // steps, r.shape[1]), lambda i: (i, 0))
-
     return pl.pallas_call(
-        hand_over,
-        grid=(steps,),
+        functools.partial(hand_over, steps),
         out_shape=tuple(shape(r.shape, r.dtype) for r in results),
-        in_specs=[slab(r) for r in results],
-        out_specs=tuple(slab(r) for r in results),
+        in_specs=[anywhere] * 3,
+        out_specs=(anywhere,) * 3,
+        scratch_shapes=[pltpu.VMEM(r.shape, r.dtype) for r in results]
+        + [pltpu.SemaphoreType.DMA((3 * steps,))] * 2,
+        compiler_params=pltpu.CompilerParams(vmem_limit_bytes=60 * 2**20),
         cost_estimate=pl.CostEstimate(
             flops=0, bytes_accessed=6 * values.size * 2, transcendentals=0
         ),

time: 236 us -> 240 us (1.017)
  the two profiles are of different devices: /device:TPU:21 before, /device:TPU:0 now
where the time goes in v4:
time: 240 us
  Pallas kernels  239 us (100%)
    pallas_call x1, Pallas kernels, on_device(): pl.pallas_call(functools.partial(kernel, n, nh, capacity, head_size), out...  236 us

profile of v4, /device:TPU:0, one launch (start us, length us, event | category | flops | bytes accessed | tf_op | source)
XLA Modules:
  0.0 239.8 jit_solution(5363710390518346319)
XLA Ops:
  0.6 236.3 %shard_map.85 = (bf16[512,1024]{1,0:T(8,128)(2,1)}, bf16[512,1024]{1,0:T(8,128)(2,1)}, bf16[512,1024]{1,0:T(8,128)(2,1)}) custom-call(bf16[512,1024]{1,0:T(8,128)(2,1)} %qk_hbm.1, bf16[512,1024]{1,0:T(8,128)(2,1)} %v_hbm.1, bf16[1024,2048]{1,0:T(8,128)(2,1)} %w_hbm.1, bf16[512,2048]{1,0:T(8,128)(2,1)} %og_hbm.1, s32[8,512]{1,0:T(8,128)} %sort_ref.1, ...), custom_call_target="tpu_custom_call" | custom-call | flops 20000000000 | bytes 16777216 | tf_op jit(solution)/shard_map/pallas_call | solution.py:408
  236.9 2.8 %shard_map.86 = (bf16[512,1024]{1,0:T(8,128)(2,1)}, bf16[512,1024]{1,0:T(8,128)(2,1)}, bf16[512,1024]{1,0:T(8,128)(2,1)}) custom-call(bf16[512,1024]{1,0:T(8,128)(2,1)} %get-tuple-element.6.refs_0_, bf16[512,1024]{1,0:T(8,128)(2,1)} %get-tuple-element.7.refs_1_, bf16[512,1024]{1,0:T(8,128)(2,1)} %get-tuple-element.8.refs_2_), custom_call_target="tpu_custom_call" | custom-call | bytes 6291456 | tf_op jit(solution)/shard_map/pallas_call | solution.py:462
